TPU v7x, 512 devices: a whole 4x8x8 slice. The times are simulated.
512 devices in a mesh: dom: 64 (over z, x, core), slab: 8 (over y).
Axes of the slice: x: 4, y: 8, z: 8, core: 2. Of those that a mesh axis runs over, the one named last changes fastest.
Arguments:
- density_map: float32 [64, 512, 1024], P('dom', None, 'slab'), may hold values from 0.1 to 12
- offsets: float32 [3, 64, 8, 512], P(None, 'dom', 'slab'), may hold values from 0 to 1
- velocities: float32 [3, 64, 8, 512], P(None, 'dom', 'slab'), may hold values from -1.2 to 1.2
- weights: float32 [64, 8, 512], P('dom', 'slab'), may hold values from 1 to 16
- atom_cells: int32 [3, 64, 8, 512], P(None, 'dom', 'slab'), may hold values from 0 to 1020, as said below
- pair_tiles: int32 [64, 8, 2, 3], P('dom', 'slab'), may hold values from 0 to 3, as said below
- halo_lists: int32 [64, 8, 4, 128], P('dom', 'slab'), may hold values from 0 to 511, as said below
Outputs:
- displacement: float32 [3, 64, 8, 512], P(None, 'dom', 'slab')
- final_velocities: float32 [3, 64, 8, 512], P(None, 'dom', 'slab')
Inputs may be any that keep to these rules, and one draw needn't show every extreme that they name: `atom_cells`: an atom of the device at dom index d and slab index s has x cell in [3, 61), y cell in [d * 8, (d + 1) * 8) and z cell in [s * 128 + 3, (s + 1) * 128 - 3). `pair_tiles`: row b of a device starts with b itself, then names distinct other source blocks; sources 2 and 3 are the rim atoms. `halo_lists`: each list holds 128 distinct atoms of the device.
All inputs are finite; a program needn't handle non-finite values.
Results may differ from a plain program's by a relative error of at most 0.017.
Values may be sent and summed in bfloat16 or wider, within the bound.
A program may use at most 128 MiB of HBM per device.

v0:
```python
import math

import jax
import jax.numpy as jnp
from jax import lax
from jax.sharding import PartitionSpec as P

REACH = 3
BLOCK = 256
BLOCKS = 2
STEPS = 3


FORCE_GAIN = 2.0
PAIR_GAIN = 0.1
PAIR_SOFT = 64.0
TIME_STEP = 0.25


def from_behind(value, axis, steps):
    count = lax.axis_size(axis)
    leading, last = (max(0, -steps), min(count, count - steps))
    return lax.ppermute(value, axis, [(source, source + steps) for source in range(leading, last)])


def stencil_rows(offset, reach):
    spacing = (jnp.arange(2 * reach + 1) - reach).astype(jnp.float32)[:, None] - offset[None, :]
    values = jnp.exp(-0.5 * spacing * spacing)
    return (values, values * spacing)


def expand_rows(values, first, length):
    relative = jnp.arange(length, dtype=jnp.int32)[:, None] - first[None, :]
    total = jnp.zeros((length, values.shape[1]), jnp.float32)
    for offset_index in range(values.shape[0]):
        total = total + jnp.where(
            relative == offset_index, values[offset_index][None, :], jnp.float32(0.0)
        )
    return total


def atom_factors(moved, cells, x_first, x_length, y_cells, z_cells, reach):
    x_vals, x_slopes = stencil_rows(moved[0], reach)
    y_vals, y_slopes = stencil_rows(moved[1], reach)
    z_vals, z_slopes = stencil_rows(moved[2], reach)
    x_start = cells[0] - reach - x_first
    y_start = cells[1] % y_cells
    z_start = cells[2] % z_cells - reach
    x_factors = jnp.concatenate(
        [expand_rows(x_vals, x_start, x_length), expand_rows(x_slopes, x_start, x_length)], axis=1
    ).astype(jnp.bfloat16)
    y_width = y_cells + 2 * reach
    y_parts = (expand_rows(y_vals, y_start, y_width), expand_rows(y_slopes, y_start, y_width))
    z_parts = (expand_rows(z_vals, z_start, z_cells), expand_rows(z_slopes, z_start, z_cells))
    return (x_factors, y_parts, z_parts)


def spread_block(x_factors, y_parts, z_parts, weights):
    count = weights.shape[0]
    cross = (weights[None, None, :] * y_parts[0][:, None, :] * z_parts[0][None, :, :]).astype(
        jnp.bfloat16
    )
    cross = cross.reshape(-1, count)
    return lax.dot_general(
        x_factors[:, :count], cross, (((1,), (1,)), ((), ())), preferred_element_type=jnp.float32
    )


def pull_block(window, x_factors, y_parts, z_parts, weights):
    count = weights.shape[0]
    pulled = lax.dot_general(
        window, x_factors, (((0,), (0,)), ((), ())), preferred_element_type=jnp.float32
    )
    pulled = pulled.reshape(y_parts[0].shape[0], z_parts[0].shape[0], 2 * count)
    plain = pulled[:, :, :count]
    sloped = pulled[:, :, count:]
    plain_z = jnp.sum(plain * z_parts[0][None], axis=1)
    sloped_z = jnp.sum(sloped * z_parts[0][None], axis=1)
    plain_dz = jnp.sum(plain * z_parts[1][None], axis=1)
    force_x = jnp.sum(sloped_z * y_parts[0], axis=0)
    force_y = jnp.sum(plain_z * y_parts[1], axis=0)
    force_z = jnp.sum(plain_dz * y_parts[0], axis=0)
    return weights[None, :] * jnp.stack([force_x, force_y, force_z])


def pair_block_forces(targets, target_weights, sources, source_weights, tiles, block):
    results = []
    for block_index in range(tiles.shape[0]):
        near = targets[:, block_index * block : (block_index + 1) * block]
        near_weights = target_weights[block_index * block : (block_index + 1) * block]
        total = jnp.zeros((3, block), jnp.float32)
        for tile_index in range(tiles.shape[1]):
            start = tiles[block_index, tile_index] * block
            far = lax.dynamic_slice_in_dim(sources, start, block, 1)
            far_weights = lax.dynamic_slice_in_dim(source_weights, start, block, 0)
            between = near[:, :, None] - far[:, None, :]
            squared = jnp.sum(between * between, axis=0) + PAIR_SOFT
            falloff = far_weights[None, :] / (squared * jnp.sqrt(squared))
            total = total + jnp.sum(between * falloff[None], axis=2)
        results.append(PAIR_GAIN * near_weights[None, :] * total)
    return jnp.concatenate(results, axis=1)


def fold_rims(received, y_cells, reach):
    core = received[:, :, reach : reach + y_cells]
    upper_rims = received[:, :, reach + y_cells :]
    lower_rims = received[:, :, :reach]
    empty = jnp.zeros_like(upper_rims[:, :1])
    from_below = jnp.concatenate([empty, upper_rims[:, :-1]], axis=1)
    from_above = jnp.concatenate([lower_rims[:, 1:], empty], axis=1)
    core = core.at[:, :, :reach].add(from_below)
    return core.at[:, :, y_cells - reach :].add(from_above)


def gradient_windows(gradient, domains, y_cells, reach):
    x_owned = gradient.shape[0]
    z_cells = gradient.shape[2]
    cores = gradient.reshape(x_owned, domains, y_cells, z_cells)
    empty = jnp.zeros((x_owned, 1, reach, z_cells), gradient.dtype)
    below = jnp.concatenate([empty, cores[:, :-1, y_cells - reach :]], axis=1)
    above = jnp.concatenate([cores[:, 1:, :reach], empty], axis=1)
    return jnp.concatenate([below, cores, above], axis=2).reshape(
        x_owned, domains * (y_cells + 2 * reach), z_cells
    )


def per_device(density_map, offsets, velocities, weights, atom_cells, pair_tiles, halo_lists):
    domains = lax.axis_size("dom")
    slabs = lax.axis_size("slab")
    x_owned = density_map.shape[0]
    y_total = density_map.shape[1]
    z_cells = density_map.shape[2]
    y_cells = y_total // domains
    x_total = x_owned * domains
    atom_count = offsets.shape[3]
    y_width = y_cells + 2 * REACH
    scale = FORCE_GAIN * math.sqrt(
        float(x_total * y_total * (z_cells * slabs) * (atom_count * domains * slabs))
    )
    base = offsets.reshape(3, atom_count)
    cells = atom_cells.reshape(3, atom_count)
    own_weights = weights.reshape(atom_count)
    speed = velocities.reshape(3, atom_count)
    tiles = pair_tiles.reshape(pair_tiles.shape[2], pair_tiles.shape[3])
    lists = halo_lists.reshape(4, halo_lists.shape[3])
    shifted = jnp.zeros((3, atom_count), jnp.float32)
    map_square = jnp.sum(density_map * density_map)
    for step_index in range(STEPS):
        moved = base + shifted
        positions = cells.astype(jnp.float32) + moved
        partial_value = jnp.zeros((x_total, y_width * z_cells), jnp.float32)
        factor_list = []
        for block_index in range(BLOCKS):
            lower = block_index * BLOCK
            factors = atom_factors(
                moved[:, lower : lower + BLOCK],
                cells[:, lower : lower + BLOCK],
                0,
                x_total,
                y_cells,
                z_cells,
                REACH,
            )
            factor_list.append(factors)
            partial_value = partial_value + spread_block(
                factors[0], factors[1], factors[2], own_weights[lower : lower + BLOCK]
            )
        received = lax.all_to_all(
            partial_value.reshape(x_total, y_width, z_cells).astype(jnp.bfloat16),
            "dom",
            split_axis=0,
            concat_axis=1,
            tiled=True,
        ).astype(jnp.float32)
        rho = fold_rims(
            received.reshape(x_owned, domains, y_width, z_cells), y_cells, REACH
        ).reshape(x_owned, y_total, z_cells)
        cross_sum, rho_square, map_total = lax.psum(
            (jnp.sum(rho * density_map), jnp.sum(rho * rho), map_square), ("dom", "slab")
        )
        norm = jnp.sqrt(rho_square * map_total)
        gradient = (density_map / norm - rho * (cross_sum / (norm * rho_square))).astype(
            jnp.bfloat16
        )
        windows = gradient_windows(gradient, domains, y_cells, REACH)
        window = lax.all_to_all(windows, "dom", split_axis=1, concat_axis=0, tiled=True).reshape(
            x_total, y_width * z_cells
        )
        pieces = []
        for block_index in range(BLOCKS):
            lower = block_index * BLOCK
            factors = factor_list[block_index]
            pieces.append(
                pull_block(
                    window, factors[0], factors[1], factors[2], own_weights[lower : lower + BLOCK]
                )
            )
        density_force = jnp.concatenate(pieces, axis=1)
        send_positions = positions[:, lists]
        send_weights = own_weights[lists]
        rims = []
        for offset_sign, entry in ((1, 1), (-1, 0)):
            rims.append(
                from_behind((send_positions[:, entry], send_weights[entry]), "dom", offset_sign)
            )
        for offset_sign, entry in ((1, 3), (-1, 2)):
            rims.append(
                from_behind((send_positions[:, entry], send_weights[entry]), "slab", offset_sign)
            )
        sources = jnp.concatenate([positions] + [member_rim[0] for member_rim in rims], axis=1)
        source_weights = jnp.concatenate(
            [own_weights] + [member_rim[1] for member_rim in rims], axis=0
        )
        pair_force = pair_block_forces(
            positions, own_weights, sources, source_weights, tiles, BLOCK
        )
        force = scale * density_force + pair_force
        speed = speed + TIME_STEP * force
        shifted = shifted + TIME_STEP * speed
    return (shifted.reshape(3, 1, 1, atom_count), speed.reshape(3, 1, 1, atom_count))


def solution(mesh):
    return jax.shard_map(
        per_device,
        mesh=mesh,
        in_specs=(
            P("dom", None, "slab"),
            P(None, "dom", "slab", None),
            P(None, "dom", "slab", None),
            P("dom", "slab", None),
            P(None, "dom", "slab", None),
            P("dom", "slab", None, None),
            P("dom", "slab", None, None),
        ),
        out_specs=(P(None, "dom", "slab", None), P(None, "dom", "slab", None)),
        check_vma=False,
    )
```

profile of v0, /device:TPU:1, one launch (start us, length us, event | category | flops | bytes accessed | tf_op | source)
XLA Modules:
  0.0 516.9 jit_solution(12629324048991010677)
XLA Ops:
  2.3 1.0 gather_fusion
  3.4 4.5 collective-permute-start
  7.9 5.6 %collective-permute-start.1 = (f32[3,128]{1,0:T(4,128)S(1)}, f32[3,128]{1,0:T(4,128)S(1)}, u32[]{:S(2)}, u32[]{:S(2)}) collective-permute-start(f32[3,128]{1,0:T(4,128)S(1)} %get-tuple-element.487), channel_id=1, source_target_pairs={{8,0},{16,8},{24,16},{32,24},{40,32},{48,40},{56,48},{64,56},{72,6... | collective-permute-start | bytes 4616 | tf_op jit(solution)/shard_map/ppermute | solution.py:23
  13.5 1.3 collective-permute-start.2
  14.8 1.3 collective-permute-start.3
  16.1 3.5 gather_fusion.1
  19.6 2.2 collective-permute-start.4
  23.8 0.9 convert_element_type.171
  24.7 15.5 %all-to-all-start = ((bf16[64,14,128]{2,1,0:T(8,128)(2,1)}), bf16[64,14,128]{2,1,0:T(8,128)(2,1)S(1)}, u32[]{:S(2)}, u32[]{:S(2)}) async-start(bf16[64,14,128]{2,1,0:T(8,128)(2,1)} %convert_element_type.171), calls=%async_computation | async-start | bytes 524288 | tf_op jit(solution)/shard_map/all_to_all | solution.py:168
  45.0 2.4 collective-permute-start.5
  47.4 2.8 collective-permute-done.5
  50.2 4.3 collective-permute-start.6
  55.1 1.3 collective-permute-start.7
  56.4 3.2 collective-permute-done.7
  64.4 103.3 %all-reduce.14 = (f32[]{:T(128)}, f32[]{:T(128)}, f32[]{:T(128)}) all-reduce(f32[]{:T(128)} %get-tuple-element.97, f32[]{:T(128)} %multiply_reduce_fusion.15, f32[]{:T(128)} %get-tuple-element.96), channel_id=1, replica_groups=mesh['dom'=64,'slab'=8] {'dom','slab'}, use_global_device_ids=true, to_apply=%region_5.6 | all-reduce | flops 3 | bytes 24 | tf_op jit(solution)/shard_map/psum | solution.py:178
  171.4 2.0 reduce.21
  173.4 0.8 reshape.4058
  174.2 7.7 %all-to-all-start.1 = ((bf16[64,2,896]{2,1,0:T(2,128)(2,1)}), bf16[64,2,896]{2,1,0:T(2,128)(2,1)S(1)}, u32[]{:S(2)}, u32[]{:S(2)}) async-start(bf16[64,2,896]{2,1,0:T(2,128)(2,1)} %reshape.4058), calls=%async_computation.1 | async-start | bytes 458752 | tf_op jit(solution)/shard_map/all_to_all | solution.py:186
  182.2 12.1 %all-to-all-done.1 = bf16[64,2,896]{2,1,0:T(2,128)(2,1)S(1)} async-done(((bf16[64,2,896]{2,1,0:T(2,128)(2,1)}), bf16[64,2,896]{2,1,0:T(2,128)(2,1)S(1)}, u32[]{:S(2)}, u32[]{:S(2)}) %all-to-all-start.1) | async-done | bytes 229408 | tf_op jit(solution)/shard_map/all_to_all | solution.py:186
  194.5 1.3 bitcast_reduce_fusion.2
  198.7 1.0 gather_fusion.2
  199.9 2.5 collective-permute-start.8
  202.4 1.9 collective-permute-start.9
  206.2 0.9 convert_element_type.181
  207.1 8.3 %all-to-all-start.2 = ((bf16[64,14,128]{2,1,0:T(8,128)(2,1)}), bf16[64,14,128]{2,1,0:T(8,128)(2,1)S(1)}, u32[]{:S(2)}, u32[]{:S(2)}) async-start(bf16[64,14,128]{2,1,0:T(8,128)(2,1)} %convert_element_type.181), calls=%async_computation.2 | async-start | bytes 524288 | tf_op jit(solution)/shard_map/all_to_all | solution.py:168
  215.7 3.3 collective-permute-start.10
  219.0 1.3 collective-permute-start.11
  220.4 3.2 collective-permute-done.11
  225.6 3.0 all-to-all-done.2
  231.2 96.6 %all-reduce.13 = (f32[]{:T(128)}, f32[]{:T(128)}) all-reduce(f32[]{:T(128)} %fusion.78, f32[]{:T(128)} %multiply_reduce_fusion.13), channel_id=1, replica_groups=mesh['dom'=64,'slab'=8] {'dom','slab'}, use_global_device_ids=true, to_apply=%region_33.34 | all-reduce | flops 2 | bytes 16 | tf_op jit(solution)/shard_map/psum | solution.py:178
  330.8 2.0 reduce.22
  333.6 7.0 %all-to-all-start.3 = ((bf16[64,2,896]{2,1,0:T(2,128)(2,1)}), bf16[64,2,896]{2,1,0:T(2,128)(2,1)S(1)}, u32[]{:S(2)}, u32[]{:S(2)}) async-start(bf16[64,2,896]{2,1,0:T(2,128)(2,1)} %reshape.4060), calls=%async_computation.3 | async-start | bytes 458752 | tf_op jit(solution)/shard_map/all_to_all | solution.py:186
  340.9 12.2 %all-to-all-done.3 = bf16[64,2,896]{2,1,0:T(2,128)(2,1)S(1)} async-done(((bf16[64,2,896]{2,1,0:T(2,128)(2,1)}), bf16[64,2,896]{2,1,0:T(2,128)(2,1)S(1)}, u32[]{:S(2)}, u32[]{:S(2)}) %all-to-all-start.3) | async-done | bytes 229408 | tf_op jit(solution)/shard_map/all_to_all | solution.py:186
  353.3 1.3 bitcast_reduce_fusion.1
  357.5 1.0 gather_fusion.3
  358.6 2.5 collective-permute-start.12
  363.1 0.9 convert_element_type.190
  363.9 6.4 %all-to-all-start.4 = ((bf16[64,14,128]{2,1,0:T(8,128)(2,1)}), bf16[64,14,128]{2,1,0:T(8,128)(2,1)S(1)}, u32[]{:S(2)}, u32[]{:S(2)}) async-start(bf16[64,14,128]{2,1,0:T(8,128)(2,1)} %convert_element_type.190), calls=%async_computation.4 | async-start | bytes 524288 | tf_op jit(solution)/shard_map/all_to_all | solution.py:168
  370.7 2.4 collective-permute-start.13
  373.0 3.0 collective-permute-start.14
  376.1 1.5 collective-permute-start.15
  377.6 3.0 collective-permute-done.15
  382.7 0.8 all-to-all-done.4
  386.2 99.9 %all-reduce.12 = (f32[]{:T(128)}, f32[]{:T(128)}) all-reduce(f32[]{:T(128)} %fusion.75, f32[]{:T(128)} %multiply_reduce_fusion.12), channel_id=1, replica_groups=mesh['dom'=64,'slab'=8] {'dom','slab'}, use_global_device_ids=true, to_apply=%region_61.62 | all-reduce | flops 2 | bytes 16 | tf_op jit(solution)/shard_map/psum | solution.py:178
  489.1 2.0 reduce.23
  491.8 7.5 %all-to-all-start.5 = ((bf16[64,2,896]{2,1,0:T(2,128)(2,1)}), bf16[64,2,896]{2,1,0:T(2,128)(2,1)S(1)}, u32[]{:S(2)}, u32[]{:S(2)}) async-start(bf16[64,2,896]{2,1,0:T(2,128)(2,1)} %reshape.4062), calls=%async_computation.5 | async-start | bytes 458752 | tf_op jit(solution)/shard_map/all_to_all | solution.py:186
  499.7 12.2 %all-to-all-done.5 = bf16[64,2,896]{2,1,0:T(2,128)(2,1)S(1)} async-done(((bf16[64,2,896]{2,1,0:T(2,128)(2,1)}), bf16[64,2,896]{2,1,0:T(2,128)(2,1)S(1)}, u32[]{:S(2)}, u32[]{:S(2)}) %all-to-all-start.5) | async-done | bytes 229408 | tf_op jit(solution)/shard_map/all_to_all | solution.py:186
  512.0 1.3 bitcast_reduce_fusion
  (266 shorter events, 36.9 us)
Async XLA Ops:
  0.6 21.2 %copy-start.2 = (s32[3,1,1,512]{3,2,1,0:T(1,128)S(1)}, s32[3,1,1,512]{3,2,1,0:T(1,128)}, u32[]{:S(2)}) copy-start(s32[3,1,1,512]{3,2,1,0:T(1,128)} %param.23) | copy-start | bytes 18436
  0.6 21.2 %copy-start.3 = (f32[3,1,1,512]{3,2,1,0:T(1,128)S(1)}, f32[3,1,1,512]{3,2,1,0:T(1,128)}, u32[]{:S(2)}) copy-start(f32[3,1,1,512]{3,2,1,0:T(1,128)} %param.20) | copy-start | bytes 18436
  0.7 15.5 %copy-start = (f32[1,1,512]{2,1,0:T(1,128)S(1)}, f32[1,1,512]{2,1,0:T(1,128)}, u32[]{:S(2)}) copy-start(f32[1,1,512]{2,1,0:T(1,128)} %param.22) | copy-start | bytes 6148
  3.4 56.3 %collective-permute-start = (f32[3,128]{1,0:T(4,128)S(1)}, f32[3,128]{1,0:T(4,128)S(1)}, u32[]{:S(2)}, u32[]{:S(2)}) collective-permute-start(f32[3,128]{1,0:T(4,128)S(1)} %get-tuple-element.488), channel_id=1, source_target_pairs={{0,8},{8,16},{16,24},{24,32},{32,40},{40,48},{48,56},{56,64},{64,7... | collective-permute-start | bytes 4616 | tf_op jit(solution)/shard_map/ppermute | solution.py:23
  7.9 51.8 %collective-permute-start.1 = (f32[3,128]{1,0:T(4,128)S(1)}, f32[3,128]{1,0:T(4,128)S(1)}, u32[]{:S(2)}, u32[]{:S(2)}) collective-permute-start(f32[3,128]{1,0:T(4,128)S(1)} %get-tuple-element.487), channel_id=1, source_target_pairs={{8,0},{16,8},{24,16},{32,24},{40,32},{48,40},{56,48},{64,56},{72,6... | collective-permute-start | bytes 4616 | tf_op jit(solution)/shard_map/ppermute | solution.py:23
  13.5 46.2 %collective-permute-start.2 = (f32[3,128]{1,0:T(4,128)S(1)}, f32[3,128]{1,0:T(4,128)S(1)}, u32[]{:S(2)}, u32[]{:S(2)}) collective-permute-start(f32[3,128]{1,0:T(4,128)S(1)} %get-tuple-element.486), channel_id=1, source_target_pairs={{0,1},{1,2},{2,3},{3,4},{4,5},{5,6},{6,7},{8,9},{9,10},{10,11},{11... | collective-permute-start | bytes 4616 | tf_op jit(solution)/shard_map/ppermute | solution.py:23
  14.8 45.0 %collective-permute-start.3 = (f32[3,128]{1,0:T(4,128)S(1)}, f32[3,128]{1,0:T(4,128)S(1)}, u32[]{:S(2)}, u32[]{:S(2)}) collective-permute-start(f32[3,128]{1,0:T(4,128)S(1)} %get-tuple-element.485), channel_id=1, source_target_pairs={{1,0},{2,1},{3,2},{4,3},{5,4},{6,5},{7,6},{9,8},{10,9},{11,10},{12... | collective-permute-start | bytes 4616 | tf_op jit(solution)/shard_map/ppermute | solution.py:23
  19.6 25.4 %collective-permute-start.4 = (f32[128]{0:T(128)S(1)}, f32[128]{0:T(128)S(1)}, u32[]{:S(2)}, u32[]{:S(2)}) collective-permute-start(f32[128]{0:T(128)S(1)} %get-tuple-element.508), channel_id=1, source_target_pairs={{0,8},{8,16},{16,24},{24,32},{32,40},{40,48},{48,56},{56,64},{64,7... | collective-permute-start | bytes 1544 | tf_op jit(solution)/shard_map/ppermute | solution.py:23
  23.0 17.2 %copy-start.5 = (s32[1,1,2,3]{3,2,1,0:T(2,128)S(1)}, s32[1,1,2,3]{3,2,1,0:T(2,128)}, u32[]{:S(2)}) copy-start(s32[1,1,2,3]{3,2,1,0:T(2,128)} %param.24) | copy-start | bytes 76
  24.7 37.4 %all-to-all-start = ((bf16[64,14,128]{2,1,0:T(8,128)(2,1)}), bf16[64,14,128]{2,1,0:T(8,128)(2,1)S(1)}, u32[]{:S(2)}, u32[]{:S(2)}) async-start(bf16[64,14,128]{2,1,0:T(8,128)(2,1)} %convert_element_type.171), calls=%async_computation | async-start | bytes 524288 | tf_op jit(solution)/shard_map/all_to_all | solution.py:168
  45.0 5.2 collective-permute-start.5
  50.2 5.0 collective-permute-start.6
  55.1 4.5 collective-permute-start.7
  62.0 1.8 copy-start.1
  174.2 20.1 %all-to-all-start.1 = ((bf16[64,2,896]{2,1,0:T(2,128)(2,1)}), bf16[64,2,896]{2,1,0:T(2,128)(2,1)S(1)}, u32[]{:S(2)}, u32[]{:S(2)}) async-start(bf16[64,2,896]{2,1,0:T(2,128)(2,1)} %reshape.4058), calls=%async_computation.1 | async-start | bytes 458752 | tf_op jit(solution)/shard_map/all_to_all | solution.py:186
  197.8 0.7 copy-start.4
  199.9 20.4 %collective-permute-start.8 = (f32[3,128]{1,0:T(4,128)S(1)}, f32[3,128]{1,0:T(4,128)S(1)}, u32[]{:S(2)}, u32[]{:S(2)}) collective-permute-start(f32[3,128]{1,0:T(4,128)S(1)} %get-tuple-element.386), channel_id=1, source_target_pairs={{0,8},{8,16},{16,24},{24,32},{32,40},{40,48},{48,56},{56,64},{64,7... | collective-permute-start | bytes 4616 | tf_op jit(solution)/shard_map/ppermute | solution.py:23
  202.4 17.9 %collective-permute-start.9 = (f32[3,128]{1,0:T(4,128)S(1)}, f32[3,128]{1,0:T(4,128)S(1)}, u32[]{:S(2)}, u32[]{:S(2)}) collective-permute-start(f32[3,128]{1,0:T(4,128)S(1)} %get-tuple-element.385), channel_id=1, source_target_pairs={{8,0},{16,8},{24,16},{32,24},{40,32},{48,40},{56,48},{64,56},{72,6... | collective-permute-start | bytes 4616 | tf_op jit(solution)/shard_map/ppermute | solution.py:23
  207.1 21.5 %all-to-all-start.2 = ((bf16[64,14,128]{2,1,0:T(8,128)(2,1)}), bf16[64,14,128]{2,1,0:T(8,128)(2,1)S(1)}, u32[]{:S(2)}, u32[]{:S(2)}) async-start(bf16[64,14,128]{2,1,0:T(8,128)(2,1)} %convert_element_type.181), calls=%async_computation.2 | async-start | bytes 524288 | tf_op jit(solution)/shard_map/all_to_all | solution.py:168
  215.7 4.6 collective-permute-start.10
  219.0 4.6 collective-permute-start.11
  333.6 19.5 %all-to-all-start.3 = ((bf16[64,2,896]{2,1,0:T(2,128)(2,1)}), bf16[64,2,896]{2,1,0:T(2,128)(2,1)S(1)}, u32[]{:S(2)}, u32[]{:S(2)}) async-start(bf16[64,2,896]{2,1,0:T(2,128)(2,1)} %reshape.4060), calls=%async_computation.3 | async-start | bytes 458752 | tf_op jit(solution)/shard_map/all_to_all | solution.py:186
  358.6 18.9 %collective-permute-start.12 = (f32[3,128]{1,0:T(4,128)S(1)}, f32[3,128]{1,0:T(4,128)S(1)}, u32[]{:S(2)}, u32[]{:S(2)}) collective-permute-start(f32[3,128]{1,0:T(4,128)S(1)} %get-tuple-element.290), channel_id=1, source_target_pairs={{0,8},{8,16},{16,24},{24,32},{32,40},{40,48},{48,56},{56,64},{64,7... | collective-permute-start | bytes 4616 | tf_op jit(solution)/shard_map/ppermute | solution.py:23
  363.9 19.6 %all-to-all-start.4 = ((bf16[64,14,128]{2,1,0:T(8,128)(2,1)}), bf16[64,14,128]{2,1,0:T(8,128)(2,1)S(1)}, u32[]{:S(2)}, u32[]{:S(2)}) async-start(bf16[64,14,128]{2,1,0:T(8,128)(2,1)} %convert_element_type.190), calls=%async_computation.4 | async-start | bytes 524288 | tf_op jit(solution)/shard_map/all_to_all | solution.py:168
  370.7 7.0 %collective-permute-start.13 = (f32[3,128]{1,0:T(4,128)S(1)}, f32[3,128]{1,0:T(4,128)S(1)}, u32[]{:S(2)}, u32[]{:S(2)}) collective-permute-start(f32[3,128]{1,0:T(4,128)S(1)} %get-tuple-element.289), channel_id=1, source_target_pairs={{8,0},{16,8},{24,16},{32,24},{40,32},{48,40},{56,48},{64,56},{72,6... | collective-permute-start | bytes 4616 | tf_op jit(solution)/shard_map/ppermute | solution.py:23
  373.0 4.6 collective-permute-start.14
  376.1 4.6 collective-permute-start.15
  491.8 20.0 %all-to-all-start.5 = ((bf16[64,2,896]{2,1,0:T(2,128)(2,1)}), bf16[64,2,896]{2,1,0:T(2,128)(2,1)S(1)}, u32[]{:S(2)}, u32[]{:S(2)}) async-start(bf16[64,2,896]{2,1,0:T(2,128)(2,1)} %reshape.4062), calls=%async_computation.5 | async-start | bytes 458752 | tf_op jit(solution)/shard_map/all_to_all | solution.py:186
where the time goes:
time: 526 us; the launch traced here: 517 us
  blocking collectives  300 us (57%)
  starting transfers between devices  93.4 us (18%)
  waiting for transfers between devices  53.2 us (10%)
  other arithmetic  27.3 us (5%)
  local copies, waits for them, and re-layouts  22.4 us (4%)
  between operations  14.2 us (3%)
  matrix products  6.46 us (1%)
    psum x3, blocking collectives, per_device(): lax.psum((jnp.sum(rho * density_map), jnp.sum(rho * rho), map_square), ('...  300 us
    ppermute x16, starting transfers between devices, from_behind(): lax.ppermute(value, axis, [(source, source + steps) for source in range(l...  41.1 us
    all_to_all x3, waiting for transfers between devices, per_device(): lax.all_to_all(windows, 'dom', split_axis=1, concat_axis=0, tiled=True)  36.4 us
    all_to_all x3, starting transfers between devices, per_device(): lax.all_to_all(partial_value.reshape(x_total, y_width, z_cells).astype(jn...  30.2 us
    all_to_all x3, starting transfers between devices, per_device(): lax.all_to_all(windows, 'dom', split_axis=1, concat_axis=0, tiled=True)  22.1 us
    ppermute x16, waiting for transfers between devices, from_behind(): lax.ppermute(value, axis, [(source, source + steps) for source in range(l...  12.9 us
  transfers between devices with their start and end apart: 22, of which 10 were waited for; matrix products, arithmetic and copies ran while one was open for 4% of the time, Pallas kernels for 0%

commit v1 on v0

v1 whole, which is shorter than its diff:
```python
import functools
import math

import jax
import jax.numpy as jnp
from jax import lax
from jax.experimental import pallas as pl
from jax.experimental.pallas import tpu as pltpu
from jax.sharding import PartitionSpec as P

REACH = 3
BLOCK = 256
BLOCKS = 2
TILES_PER = 3
STEPS = 3
ATOMS = 512
HALO = 128
DOMAINS = 64
SLABS = 8
X_CELLS = 64
Y_CELLS = 8
Z_CELLS = 128
ROWS = 16
BELOW = 4
Z_CHIPS, X_CHIPS, CORES = 8, 4, 2

FORCE_GAIN = 2.0
PAIR_GAIN = 0.1
PAIR_SOFT = 64.0
TIME_STEP = 0.25
SCALE = FORCE_GAIN * math.sqrt(float(X_CELLS * Y_CELLS * DOMAINS * Z_CELLS * SLABS * ATOMS * DOMAINS * SLABS))

MESH = pl.DeviceIdType.MESH
F32, BF16 = jnp.float32, jnp.bfloat16
BASE, U, V, CELL, WEIGHT, RECORD = 0, 3, 6, 9, 12, 16
LOWER, UPPER = 0, 1


def for_dom_peers(dom, do):
    z, x, core = dom // (X_CHIPS * CORES), dom // CORES % X_CHIPS, dom % CORES

    def along_x(dz):
        for dx in (2, 1, 3, 0):
            for dc in (1, 0):
                if isinstance(dz, int) and dz + dx + dc == 0:
                    continue
                peer = ((z + dz) % Z_CHIPS * X_CHIPS + (x + dx) % X_CHIPS) * CORES + (core + dc) % CORES
                do((dz * X_CHIPS + dx) * CORES + dc - 1, peer)

    def body(j, carry):
        along_x(Z_CHIPS // 2 + (1 - 2 * (j % 2)) * ((j + 1) // 2))
        return carry

    lax.fori_loop(0, Z_CHIPS - 1, body, 0)
    along_x(0)


def for_slab_peers(slab, do):
    for k in (4, 3, 5, 2, 6, 1, 7):
        do(k - 1, (slab + k) % SLABS)


def total_of(ref, count):
    sums = []
    for first in range(0, count, 16):
        sums.append(jnp.sum(ref[first : min(first + 16, count)], axis=0))
    return functools.reduce(jnp.add, sums)


def stencil(cell, moved, index):
    steps = index - cell
    spacing = steps - moved
    values = jnp.where(jnp.abs(steps) <= float(REACH), jnp.exp(-0.5 * spacing * spacing), 0.0)
    return values, values * spacing


def float_iota(shape, dim):
    return lax.broadcasted_iota(jnp.int32, shape, dim).astype(F32)


def kernel(
    map_ref, offsets_ref, velocities_ref, weights_ref, cells_ref, tiles_ref, lists_ref,
    moved_out, speed_out,
    padded, map_send, map_recv, map_rows, windows, rho,
    records, record_recv, xf_pair, xf_pull, y_own, ys_own, y_near, z_near, zs_own,
    one_hot, rim_send, rim_recv, sources, state, pulls, ab, map_square,
    sums_send, dom_recv, slab_send, slab_recv,
    map_ssem, map_rsem, rec_ssem, rec_rsem, rim_ssem, rim_rsem, dom_ssem, dom_rsem, slab_ssem, slab_rsem,
):
    dom, slab = lax.axis_index("dom"), lax.axis_index("slab")
    lower, upper = (dom + DOMAINS - 1) % DOMAINS, (dom + 1) % DOMAINS
    before, after = (slab + SLABS - 1) % SLABS, (slab + 1) % SLABS

    barrier = pltpu.get_barrier_semaphore()

    def greet(k, carry):
        pl.semaphore_signal(barrier, inc=1, device_id=((dom + k) % DOMAINS, slab), device_id_type=MESH)
        return carry

    lax.fori_loop(1, DOMAINS, greet, 0)
    for k in range(1, SLABS):
        pl.semaphore_signal(barrier, inc=1, device_id=(dom, (slab + k) % SLABS), device_id_type=MESH)

    padded[0:8] = jnp.zeros((8, Z_CELLS), F32)
    padded[512:520] = jnp.zeros((8, Z_CELLS), F32)
    own_map = map_ref[0]
    padded[BELOW : BELOW + 512] = own_map
    square = own_map * own_map
    square = jnp.sum(jnp.sum(square.reshape(64, 8, Z_CELLS), axis=0), axis=0, keepdims=True)
    map_square[...] = square + pltpu.roll(square, 64, 1)

    def cut(t, carry):
        first = pl.multiple_of(t * Y_CELLS, Y_CELLS)
        map_send[t] = padded[pl.ds(first, ROWS)].astype(BF16)
        return carry

    lax.fori_loop(0, DOMAINS, cut, 0, unroll=8)
    map_recv[dom] = map_send[dom]

    weights = weights_ref[0]
    zero_row = jnp.zeros((1, ATOMS), F32)
    cell_rows = [cells_ref[i, 0].astype(F32) for i in range(3)]
    local_rows = [
        cell_rows[0],
        (cells_ref[1, 0] - dom * Y_CELLS).astype(F32),
        (cells_ref[2, 0] - slab * Z_CELLS).astype(F32),
    ]
    offset_rows = [offsets_ref[i, 0] for i in range(3)]
    fixed = local_rows + [weights] + [zero_row] * (RECORD - WEIGHT - 1)
    records[0] = jnp.concatenate(offset_rows + [zero_row] * 6 + fixed, axis=0)
    for i in range(3):
        state[i : i + 1] = zero_row
        state[3 + i : 4 + i] = velocities_ref[i, 0]
    ab[...] = jnp.zeros((8, ATOMS), F32)
    atom_index = lax.broadcasted_iota(jnp.int32, (ATOMS, HALO), 0)
    for entry in range(4):
        one_hot[:, entry * HALO : (entry + 1) * HALO] = jnp.where(
            atom_index == lists_ref[0, 0, entry : entry + 1, :], 1.0, 0.0
        ).astype(BF16)

    pl.semaphore_wait(barrier, DOMAINS - 1 + SLABS - 1)

    def record_copy(step, slot, peer):
        return pltpu.make_async_remote_copy(
            src_ref=records.at[step],
            dst_ref=record_recv.at[step, slot],
            send_sem=rec_ssem.at[step, slot],
            recv_sem=rec_rsem.at[step, slot],
            device_id=(peer, slab),
            device_id_type=MESH,
        )

    def send_records(step):
        record_copy(step, UPPER, lower).start()
        record_copy(step, LOWER, upper).start()

    send_records(0)

    def send_map(slot, peer):
        pltpu.make_async_remote_copy(
            src_ref=map_send.at[peer],
            dst_ref=map_recv.at[dom],
            send_sem=map_ssem,
            recv_sem=map_rsem,
            device_id=(peer, slab),
            device_id_type=MESH,
        ).start()

    for_dom_peers(dom, send_map)

    def step_body(step, carry):
        a_row, b_row = ab[0:1], ab[1:2]
        record_copy(step, LOWER, upper).wait_recv()
        record_copy(step, UPPER, lower).wait_recv()

        row = lax.broadcasted_iota(jnp.int32, (ROWS, ATOMS), 0)
        first_row = jnp.where(dom == 0, BELOW, 0)
        last_row = jnp.where(dom == DOMAINS - 1, BELOW + Y_CELLS, ROWS)
        in_grid = (row >= first_row) & (row < last_row)
        y_index = row.astype(F32) - float(BELOW)
        x_index = float_iota((X_CELLS, ATOMS), 0)
        z_index = float_iota((Z_CELLS, ATOMS), 0)
        own_moved = []
        for kind in range(3):
            record = records[step] if kind == 0 else record_recv[step, kind - 1]
            moved = [
                record[BASE + i : BASE + i + 1]
                + a_row * record[U + i : U + i + 1]
                + b_row * record[V + i : V + i + 1]
                for i in range(3)
            ]
            cell = [record[CELL + i : CELL + i + 1] for i in range(3)]
            heavy = record[WEIGHT : WEIGHT + 1]
            xv, xs = stencil(cell[0], moved[0], x_index)
            shift = (0.0, -float(Y_CELLS), float(Y_CELLS))[kind]
            yv, ys = stencil(cell[1] + shift, moved[1], y_index)
            zv, zs = stencil(cell[2], moved[2], z_index)
            xv = xv.astype(BF16)
            z_near[kind] = zv
            if kind == 0:
                xf_pair[0, :, 0:ATOMS] = xv
                xf_pair[1, :, 0:ATOMS] = xv
                xf_pull[:, 0:ATOMS] = xv
                xf_pull[:, ATOMS:] = xs.astype(BF16)
                zs_own[...] = zs
                y_own[...] = jnp.where(in_grid, heavy * yv, 0.0)
                ys_own[...] = heavy * ys
            else:
                xf_pair[kind - 1, :, ATOMS:] = xv
                there = (dom > 0) if kind == 1 else (dom < DOMAINS - 1)
                y_near[kind - 1] = jnp.where(in_grid & there, heavy * yv, 0.0)
            if kind == 0:
                own_moved = moved

        def spread_half(half, carry):
            def spread_row(i, carry):
                r = 1 + half * 7 + i
                cross = jnp.concatenate(
                    [
                        (y_own[pl.ds(r, 1)] * z_near[0]).astype(BF16),
                        (y_near[half, pl.ds(r, 1)] * z_near[half + 1]).astype(BF16),
                    ],
                    axis=1,
                )
                out = lax.dot_general(cross, xf_pair[half], (((1,), (1,)), ((), ())), preferred_element_type=F32)
                place = pl.ds(pl.multiple_of(r * Z_CELLS, Z_CELLS), Z_CELLS)
                rho[place] = out
                windows[1, place] = out.astype(BF16)
                return carry

            return lax.fori_loop(0, 7, spread_row, carry)

        lax.fori_loop(0, 2, spread_half, 0)

        @pl.when(step == 0)
        def _():
            everything = map_recv.at[pl.ds(0, DOMAINS - 1)]
            pltpu.make_async_copy(everything, everything, map_rsem).wait()
            map_rows[...] = map_recv[...].astype(F32).reshape(X_CELLS * ROWS, Z_CELLS)

            for r in range(ROWS):
                plane = map_rows[pl.ds(r, X_CELLS, stride=ROWS)]
                windows[0, r * Z_CELLS : (r + 1) * Z_CELLS] = plane.T.astype(BF16)

        def sum_row(r, carry):
            rr, rm = carry
            place = pl.ds(pl.multiple_of(r * Z_CELLS, Z_CELLS), Z_CELLS)
            here = rho[place].reshape(16, 8, X_CELLS)
            there = windows[0, place].astype(F32).reshape(16, 8, X_CELLS)
            return rr + jnp.sum(here * here, axis=0), rm + jnp.sum(here * there, axis=0)

        nothing = jnp.zeros((8, X_CELLS), F32)
        rr, rm = lax.fori_loop(BELOW, BELOW + Y_CELLS, sum_row, (nothing, nothing))
        both = jnp.concatenate(
            [jnp.sum(rr, axis=0, keepdims=True), jnp.sum(rm, axis=0, keepdims=True)], axis=1
        )
        both = both + pltpu.roll(both, 96, 1)
        lane = lax.broadcasted_iota(jnp.int32, (1, 128), 1)
        sums = jnp.where(lane < 64, both, map_square[...])
        sums_send[step] = jnp.where((lane >= 32) & (lane < 64), pltpu.roll(both, 96, 1), sums)

        def dom_copy(slot, peer):
            pltpu.make_async_remote_copy(
                src_ref=sums_send.at[step],
                dst_ref=dom_recv.at[step, slot],
                send_sem=dom_ssem.at[step],
                recv_sem=dom_rsem.at[step],
                device_id=(peer, slab),
                device_id_type=MESH,
            ).start()

        for_dom_peers(dom, dom_copy)

        positions = jnp.concatenate([cell_rows[i] + own_moved[i] for i in range(3)] + [weights] + [zero_row] * 4, axis=0)
        high = positions.astype(BF16).astype(F32)
        middle = (positions - high).astype(BF16).astype(F32)
        low = positions - high - middle
        split = jnp.concatenate([high, middle, low, jnp.zeros((8, ATOMS), F32)], axis=0).astype(BF16)
        listed = jnp.dot(split, one_hot[...], preferred_element_type=F32)
        listed = listed[0:8] + listed[8:16] + listed[16:24]

        def rim_copy(entry):
            slot, place = (
                (1, (lower, slab)), (0, (upper, slab)), (3, (dom, before)), (2, (dom, after)),
            )[entry]
            return pltpu.make_async_remote_copy(
                src_ref=rim_send.at[step, entry],
                dst_ref=rim_recv.at[step, slot],
                send_sem=rim_ssem.at[step, entry],
                recv_sem=rim_rsem.at[step, slot],
                device_id=place,
                device_id_type=MESH,
            )

        for entry in range(4):
            rim_send[step, entry] = listed[:, entry * HALO : (entry + 1) * HALO]
            rim_copy(entry).start()

        def pull(which, carry):
            def pull_row(r, sums):
                place = pl.ds(pl.multiple_of(r * Z_CELLS, Z_CELLS), Z_CELLS)
                window = windows[which, place]
                yv, ys = y_own[pl.ds(r, 1)], ys_own[pl.ds(r, 1)]
                out = []
                for half in range(2):
                    at = slice(half * 256, (half + 1) * 256)
                    plain = jnp.dot(window, xf_pull[:, half * 256 : (half + 1) * 256], preferred_element_type=F32)
                    sloped = jnp.dot(window, xf_pull[:, ATOMS + half * 256 : ATOMS + (half + 1) * 256], preferred_element_type=F32)
                    zv, zs = z_near[0, :, at], zs_own[:, at]

                    def over_z(product):
                        return jnp.sum(product.reshape(16, 8, 256), axis=0)

                    out.append(sums[half * 3] + over_z(sloped * zv) * yv[:, at])
                    out.append(sums[half * 3 + 1] + over_z(plain * zv) * ys[:, at])
                    out.append(sums[half * 3 + 2] + over_z(plain * zs) * yv[:, at])
                return tuple(out)

            sums = lax.fori_loop(1, ROWS - 1, pull_row, (jnp.zeros((8, 256), F32),) * 6)
            for half in range(2):
                rows = [jnp.sum(sums[half * 3 + i], axis=0, keepdims=True) for i in range(3)]
                pulls[which, :, half * 256 : (half + 1) * 256] = jnp.concatenate(rows + [jnp.zeros((5, 256), F32)], axis=0)
            return carry

        lax.fori_loop(0, 2, pull, 0)

        rims = []
        for slot in range(4):
            rim_copy((1, 0, 3, 2)[slot]).wait_recv()
            there = ((dom > 0), (dom < DOMAINS - 1), (slab > 0), (slab < SLABS - 1))[slot]
            keep = (lax.broadcasted_iota(jnp.int32, (8, HALO), 0) != 3) | there
            rims.append(jnp.where(keep, rim_recv[step, slot], 0.0))
        blocks = [positions[:, 0:BLOCK], positions[:, BLOCK:]]
        blocks += [jnp.concatenate(rims[0:2], axis=1), jnp.concatenate(rims[2:4], axis=1)]
        for block in range(BLOCKS):
            for j in range(TILES_PER):
                listed_block = blocks[block]
                if j > 0:
                    source = jnp.full((8, BLOCK), tiles_ref[0, 0, block, j], jnp.int32)
                    listed_block = blocks[3]
                    for t in range(3):
                        listed_block = jnp.where(source == t, blocks[t], listed_block)
                sources[block, j * BLOCK : (j + 1) * BLOCK] = listed_block.T
        pair_rows = []
        for block in range(BLOCKS):
            at = slice(block * BLOCK, (block + 1) * BLOCK)
            near = [positions[i : i + 1, at] for i in range(3)]

            def chunk(c, total, block=block, near=near):
                far = sources[block, pl.ds(pl.multiple_of(c * 32, 32), 32)]
                between = [near[i] - far[:, i : i + 1] for i in range(3)]
                squared = between[0] * between[0] + between[1] * between[1] + between[2] * between[2] + PAIR_SOFT
                inverse = lax.rsqrt(squared)
                falloff = far[:, 3:4] * (inverse * inverse * inverse)
                return tuple(
                    total[i] + jnp.sum((between[i] * falloff).reshape(4, 8, BLOCK), axis=0) for i in range(3)
                )

            total = lax.fori_loop(0, TILES_PER * BLOCK // 32, chunk, (jnp.zeros((8, BLOCK), F32),) * 3)
            pair_rows.append([jnp.sum(t, axis=0, keepdims=True) for t in total])

        gain = TIME_STEP * TIME_STEP * SCALE
        u_rows, v_rows, base_rows = [], [], []
        for i in range(3):
            pair = jnp.concatenate([pair_rows[block][i] for block in range(BLOCKS)], axis=1)
            speed = state[3 + i : 4 + i] + TIME_STEP * (PAIR_GAIN * weights * pair)
            state[3 + i : 4 + i] = speed
            base_rows.append(own_moved[i] + TIME_STEP * speed)
            u_rows.append(gain * pulls[0, i : i + 1])
            v_rows.append(-gain * pulls[1, i : i + 1])
        record = jnp.concatenate(base_rows + u_rows + v_rows + fixed, axis=0)

        @pl.when(step < STEPS - 1)
        def _():
            records[step + 1] = record
            send_records(step + 1)

        pltpu.make_async_copy(dom_recv.at[step], dom_recv.at[step], dom_rsem.at[step]).wait()
        slab_send[step] = sums_send[step] + total_of(dom_recv.at[step], DOMAINS - 1)

        def slab_copy(slot, peer):
            pltpu.make_async_remote_copy(
                src_ref=slab_send.at[step],
                dst_ref=slab_recv.at[step, slot],
                send_sem=slab_ssem.at[step],
                recv_sem=slab_rsem.at[step],
                device_id=(dom, peer),
                device_id_type=MESH,
            ).start()

        for_slab_peers(slab, slab_copy)
        pltpu.make_async_copy(slab_recv.at[step], slab_recv.at[step], slab_rsem.at[step]).wait()
        sums = slab_send[step] + total_of(slab_recv.at[step], SLABS - 1)
        srr = jnp.sum(jnp.where(lane < 32, sums, 0.0), axis=1, keepdims=True)
        srm = jnp.sum(jnp.where((lane >= 32) & (lane < 64), sums, 0.0), axis=1, keepdims=True)
        smm = jnp.sum(jnp.where(lane >= 64, sums, 0.0), axis=1, keepdims=True)
        norm = jnp.sqrt(srr * smm)
        a = 1.0 / norm
        b = srm / (norm * srr)
        ab[0:1] = jnp.broadcast_to(a, (1, ATOMS))
        ab[1:2] = jnp.broadcast_to(b, (1, ATOMS))
        for i in range(3):
            speed = state[3 + i : 4 + i] + (a * u_rows[i] + b * v_rows[i]) * (1.0 / TIME_STEP)
            state[3 + i : 4 + i] = speed
            state[i : i + 1] = state[i : i + 1] + TIME_STEP * speed
        return carry

    lax.fori_loop(0, STEPS, step_body, 0)
    for i in range(3):
        moved_out[i, 0] = state[i : i + 1]
        speed_out[i, 0] = state[3 + i : 4 + i]

    everything = map_send.at[pl.ds(0, DOMAINS - 1)]
    pltpu.make_async_copy(everything, everything, map_ssem).wait()

    def drain(step, carry):
        record_copy(step, UPPER, lower).wait_send()
        record_copy(step, LOWER, upper).wait_send()
        for entry in range(4):
            pltpu.make_async_copy(rim_send.at[step, entry], rim_send.at[step, entry], rim_ssem.at[step, entry]).wait()
        pltpu.make_async_copy(dom_recv.at[step], dom_recv.at[step], dom_ssem.at[step]).wait()
        pltpu.make_async_copy(slab_recv.at[step], slab_recv.at[step], slab_ssem.at[step]).wait()
        return carry

    lax.fori_loop(0, STEPS, drain, 0)


def per_device(density_map, offsets, velocities, weights, atom_cells, pair_tiles, halo_lists):
    vmem = pl.BlockSpec(memory_space=pltpu.VMEM)
    smem = pl.BlockSpec(memory_space=pltpu.SMEM)
    out = jax.ShapeDtypeStruct(offsets.shape, F32)
    dma = pltpu.SemaphoreType.DMA
    scratch = [
        pltpu.VMEM((520, Z_CELLS), F32),
        pltpu.VMEM((DOMAINS, ROWS, Z_CELLS), BF16),
        pltpu.VMEM((X_CELLS, ROWS, Z_CELLS), BF16),
        pltpu.VMEM((X_CELLS * ROWS, Z_CELLS), F32),
        pltpu.VMEM((2, ROWS * Z_CELLS, X_CELLS), BF16),
        pltpu.VMEM((ROWS * Z_CELLS, X_CELLS), F32),
        pltpu.VMEM((STEPS, RECORD, ATOMS), F32),
        pltpu.VMEM((STEPS, 2, RECORD, ATOMS), F32),
        pltpu.VMEM((2, X_CELLS, 2 * ATOMS), BF16),
        pltpu.VMEM((X_CELLS, 2 * ATOMS), BF16),
        pltpu.VMEM((ROWS, ATOMS), F32),
        pltpu.VMEM((ROWS, ATOMS), F32),
        pltpu.VMEM((2, ROWS, ATOMS), F32),
        pltpu.VMEM((3, Z_CELLS, ATOMS), F32),
        pltpu.VMEM((Z_CELLS, ATOMS), F32),
        pltpu.VMEM((ATOMS, 4 * HALO), BF16),
        pltpu.VMEM((STEPS, 4, 8, HALO), F32),
        pltpu.VMEM((STEPS, 4, 8, HALO), F32),
        pltpu.VMEM((BLOCKS, TILES_PER * BLOCK, 8), F32),
        pltpu.VMEM((8, ATOMS), F32),
        pltpu.VMEM((2, 8, ATOMS), F32),
        pltpu.VMEM((8, ATOMS), F32),
        pltpu.VMEM((1, 128), F32),
        pltpu.VMEM((STEPS, 1, 128), F32),
        pltpu.VMEM((STEPS, DOMAINS - 1, 1, 128), F32),
        pltpu.VMEM((STEPS, 1, 128), F32),
        pltpu.VMEM((STEPS, SLABS - 1, 1, 128), F32),
        dma, dma,
        dma((STEPS, 2)), dma((STEPS, 2)),
        dma((STEPS, 4)), dma((STEPS, 4)),
        dma((STEPS,)), dma((STEPS,)),
        dma((STEPS,)), dma((STEPS,)),
    ]
    return pl.pallas_call(
        kernel,
        out_shape=(out, out),
        in_specs=[vmem, vmem, vmem, vmem, vmem, smem, vmem],
        out_specs=(vmem, vmem),
        scratch_shapes=scratch,
        compiler_params=pltpu.CompilerParams(
            collective_id=0, has_side_effects=True, vmem_limit_bytes=40 * 1024 * 1024
        ),
        name="density_steps",
    )(density_map, offsets, velocities, weights, atom_cells, pair_tiles, halo_lists)


def solution(mesh):
    return jax.shard_map(
        per_device,
        mesh=mesh,
        in_specs=(
            P("dom", None, "slab"),
            P(None, "dom", "slab", None),
            P(None, "dom", "slab", None),
            P("dom", "slab", None),
            P(None, "dom", "slab", None),
            P("dom", "slab", None, None),
            P("dom", "slab", None, None),
        ),
        out_specs=(P(None, "dom", "slab", None), P(None, "dom", "slab", None)),
        check_vma=False,
    )
```

time: 526 us -> 90.4 us (0.17); the launches traced: 517 us -> 89.6 us
  blocking collectives: 300 us -> 0 us
  starting transfers between devices: 93.4 us -> 0 us
  Pallas kernels: 0 us -> 82.7 us
  waiting for transfers between devices: 53.2 us -> 0 us
  other arithmetic: 27.3 us -> 0 us
  local copies, waits for them, and re-layouts: 22.4 us -> 6.25 us
  between operations: 14.2 us -> 0.66 us
  matrix products: 6.46 us -> 0 us
    psum x3 -> x0, blocking collectives: 300 us -> none  [per_device(): lax.psum((jnp.sum(rho * density_map), jnp.sum(rho * rho), map_square), ('...]
    pallas_call x0 -> x1, Pallas kernels: none -> 82.7 us  [per_device(): pl.pallas_call(kernel, out_shape=(out, out), in_specs=[vmem, vmem, vmem,...]
    all_to_all x6 -> x0, starting transfers between devices: 52.3 us -> none  [the longest x3 30.2 us: per_device(): lax.all_to_all(partial_value.reshape(x_total, y_width, z_cells).astype(jn...]
    ppermute x16 -> x0, starting transfers between devices: 41.1 us -> none  [from_behind(): lax.ppermute(value, axis, [(source, source + steps) for source in range(l...]
    all_to_all x6 -> x0, waiting for transfers between devices: 40.2 us -> none  [the longest x3 36.4 us: per_device(): lax.all_to_all(windows, 'dom', split_axis=1, concat_axis=0, tiled=True)]
    reduce_sum x35 -> x0, other arithmetic: 13 us -> none  [the longest x12 4.52 us: pair_block_forces(): total = total + jnp.sum(between * falloff[None], axis=2)]
    ppermute x16 -> x0, waiting for transfers between devices: 12.9 us -> none  [from_behind(): lax.ppermute(value, axis, [(source, source + steps) for source in range(l...]
    gather x7 -> x0, local copies, waits for them, and re-layouts: 6.92 us -> none  [the longest x1 3.49 us: per_device(): send_weights = own_weights[lists]]
  transfers between devices with their start and end apart: 22 -> 0, of which waited for: 10 -> 0; matrix products, arithmetic and copies ran while one was open for 4% -> 0% of each run, Pallas kernels for 0% -> 0%
where the time goes in v1:
time: 90.4 us; the launch traced here: 89.6 us
  Pallas kernels  82.7 us (91%)
  local copies, waits for them, and re-layouts  6.25 us (7%)
    pallas_call x1, Pallas kernels, per_device(): pl.pallas_call(kernel, out_shape=(out, out), in_specs=[vmem, vmem, vmem,...  82.7 us
    unnamed x16, local copies, waits for them, and re-layouts  6.25 us

profile of v1, /device:TPU:1, one launch (start us, length us, event | category | flops | bytes accessed | tf_op | source)
XLA Modules:
  0.0 89.6 jit_solution(12393755194024516621)
XLA Ops:
  0.6 0.0 copy-start
  0.6 0.9 %copy-done = f32[1,512,128]{2,1,0:T(8,128)S(1)} copy-done((f32[1,512,128]{2,1,0:T(8,128)S(1)}, f32[1,512,128]{2,1,0:T(8,128)}, u32[]{:S(2)}) %copy-start) | copy-done | bytes 262168
  1.6 0.0 copy-start.1
  1.6 0.7 copy-done.1
  2.3 0.0 copy-start.2
  2.3 0.7 copy-done.2
  3.0 0.0 copy-start.3
  3.0 0.7 copy-done.3
  3.7 0.0 copy-start.4
  3.7 0.7 copy-done.4
  4.3 0.0 copy-start.5
  4.3 0.7 copy-done.5
  5.0 0.0 copy-start.6
  5.0 0.7 copy-done.6
  5.7 82.7 %density_steps.1 = (f32[3,1,1,512]{3,2,1,0:T(1,128)S(1)}, f32[3,1,1,512]{3,2,1,0:T(1,128)S(1)}) custom-call(f32[1,512,128]{2,1,0:T(8,128)S(1)} %copy-done, f32[3,1,1,512]{3,2,1,0:T(1,128)S(1)} %copy-done.1, f32[3,1,1,512]{3,2,1,0:T(1,128)S(1)} %copy-done.2, f32[1,1,512]{2,1,0:T(1,128)S(1)} %copy-done.4, s32[3,1,1,512]{3,2,1,0:T(1,128)S(1)} %copy-done.3, ...), custom_call_target="tpu_custom_call" | custom-call | tf_op jit(solution)/shard_map/density_steps/pallas_call | solution.py:467
  88.4 0.6 copy.11
  89.0 0.6 copy.12
Async XLA Ops:
  0.6 1.0 %copy-start = (f32[1,512,128]{2,1,0:T(8,128)S(1)}, f32[1,512,128]{2,1,0:T(8,128)}, u32[]{:S(2)}) copy-start(f32[1,512,128]{2,1,0:T(8,128)} %map_ref.1) | copy-start | bytes 786436
  1.6 0.7 copy-start.1
  2.3 0.7 copy-start.2
  3.0 0.7 copy-start.3
  3.7 0.7 copy-start.4
  4.3 0.7 copy-start.5
  5.0 0.7 copy-start.6

commit v2 on v1

--- a/solution.py
+++ b/solution.py
@@ -79,8 +79,9 @@
 
 
 def kernel(
-    map_ref, offsets_ref, velocities_ref, weights_ref, cells_ref, tiles_ref, lists_ref,
-    moved_out, speed_out,
+    map_hbm, offsets_hbm, velocities_hbm, weights_hbm, cells_hbm, tiles_hbm, lists_hbm,
+    moved_out, speed_out, push_out,
+    map_ref, offsets_ref, velocities_ref, weights_ref, cells_ref, tiles_ref, lists_ref, fetched,
     padded, map_send, map_recv, map_rows, windows, rho,
     records, record_recv, xf_pair, xf_pull, y_own, ys_own, y_near, z_near, zs_own,
     one_hot, rim_send, rim_recv, sources, state, pulls, ab, map_square,
@@ -91,6 +92,16 @@
     lower, upper = (dom + DOMAINS - 1) % DOMAINS, (dom + 1) % DOMAINS
     before, after = (slab + SLABS - 1) % SLABS, (slab + 1) % SLABS
 
+    fetches = [
+        pltpu.make_async_copy(source, target, fetched.at[i])
+        for i, (source, target) in enumerate((
+            (map_hbm, map_ref), (offsets_hbm, offsets_ref), (velocities_hbm, velocities_ref), (weights_hbm, weights_ref),
+            (cells_hbm, cells_ref), (tiles_hbm, tiles_ref), (lists_hbm, lists_ref),
+        ))
+    ]
+    for fetch in fetches:
+        fetch.start()
+
     barrier = pltpu.get_barrier_semaphore()
 
     def greet(k, carry):
@@ -100,6 +111,9 @@
     lax.fori_loop(1, DOMAINS, greet, 0)
     for k in range(1, SLABS):
         pl.semaphore_signal(barrier, inc=1, device_id=(dom, (slab + k) % SLABS), device_id_type=MESH)
+
+    for fetch in fetches:
+        fetch.wait()
 
     padded[0:8] = jnp.zeros((8, Z_CELLS), F32)
     padded[512:520] = jnp.zeros((8, Z_CELLS), F32)
@@ -228,7 +242,7 @@
                 windows[1, place] = out.astype(BF16)
                 return carry
 
-            return lax.fori_loop(0, 7, spread_row, carry)
+            return lax.fori_loop(0, 7, spread_row, carry, unroll=7)
 
         lax.fori_loop(0, 2, spread_half, 0)
 
@@ -316,7 +330,7 @@
                     out.append(sums[half * 3 + 2] + over_z(plain * zs) * yv[:, at])
                 return tuple(out)
 
-            sums = lax.fori_loop(1, ROWS - 1, pull_row, (jnp.zeros((8, 256), F32),) * 6)
+            sums = lax.fori_loop(1, ROWS - 1, pull_row, (jnp.zeros((8, 256), F32),) * 6, unroll=7)
             for half in range(2):
                 rows = [jnp.sum(sums[half * 3 + i], axis=0, keepdims=True) for i in range(3)]
                 pulls[which, :, half * 256 : (half + 1) * 256] = jnp.concatenate(rows + [jnp.zeros((5, 256), F32)], axis=0)
@@ -336,7 +350,7 @@
             for j in range(TILES_PER):
                 listed_block = blocks[block]
                 if j > 0:
-                    source = jnp.full((8, BLOCK), tiles_ref[0, 0, block, j], jnp.int32)
+                    source = jnp.broadcast_to(tiles_ref[0, 0, block : block + 1, j : j + 1], (8, BLOCK))
                     listed_block = blocks[3]
                     for t in range(3):
                         listed_block = jnp.where(source == t, blocks[t], listed_block)
@@ -356,7 +370,7 @@
                     total[i] + jnp.sum((between[i] * falloff).reshape(4, 8, BLOCK), axis=0) for i in range(3)
                 )
 
-            total = lax.fori_loop(0, TILES_PER * BLOCK // 32, chunk, (jnp.zeros((8, BLOCK), F32),) * 3)
+            total = lax.fori_loop(0, TILES_PER * BLOCK // 32, chunk, (jnp.zeros((8, BLOCK), F32),) * 3, unroll=12)
             pair_rows.append([jnp.sum(t, axis=0, keepdims=True) for t in total])
 
         gain = TIME_STEP * TIME_STEP * SCALE
@@ -400,16 +414,16 @@
         ab[0:1] = jnp.broadcast_to(a, (1, ATOMS))
         ab[1:2] = jnp.broadcast_to(b, (1, ATOMS))
         for i in range(3):
-            speed = state[3 + i : 4 + i] + (a * u_rows[i] + b * v_rows[i]) * (1.0 / TIME_STEP)
+            push = (a * u_rows[i] + b * v_rows[i]) * (1.0 / TIME_STEP)
+            speed_out[i, 0] = state[3 + i : 4 + i]
+            push_out[i, 0] = push
+            moved_out[i, 0] = state[i : i + 1]
+            speed = state[3 + i : 4 + i] + push
             state[3 + i : 4 + i] = speed
             state[i : i + 1] = state[i : i + 1] + TIME_STEP * speed
         return carry
 
     lax.fori_loop(0, STEPS, step_body, 0)
-    for i in range(3):
-        moved_out[i, 0] = state[i : i + 1]
-        speed_out[i, 0] = state[3 + i : 4 + i]
-
     everything = map_send.at[pl.ds(0, DOMAINS - 1)]
     pltpu.make_async_copy(everything, everything, map_ssem).wait()
 
@@ -427,10 +441,13 @@
 
 def per_device(density_map, offsets, velocities, weights, atom_cells, pair_tiles, halo_lists):
     vmem = pl.BlockSpec(memory_space=pltpu.VMEM)
-    smem = pl.BlockSpec(memory_space=pltpu.SMEM)
+    hbm = pl.BlockSpec(memory_space=pltpu.HBM)
+    arguments = (density_map, offsets, velocities, weights, atom_cells, pair_tiles, halo_lists)
     out = jax.ShapeDtypeStruct(offsets.shape, F32)
     dma = pltpu.SemaphoreType.DMA
     scratch = [
+        *[pltpu.VMEM(argument.shape, argument.dtype) for argument in arguments],
+        dma((len(arguments),)),
         pltpu.VMEM((520, Z_CELLS), F32),
         pltpu.VMEM((DOMAINS, ROWS, Z_CELLS), BF16),
         pltpu.VMEM((X_CELLS, ROWS, Z_CELLS), BF16),
@@ -464,17 +481,19 @@
         dma((STEPS,)), dma((STEPS,)),
         dma((STEPS,)), dma((STEPS,)),
     ]
-    return pl.pallas_call(
+    moved, speed, push = pl.pallas_call(
         kernel,
-        out_shape=(out, out),
-        in_specs=[vmem, vmem, vmem, vmem, vmem, smem, vmem],
-        out_specs=(vmem, vmem),
+        out_shape=(out, out, out),
+        in_specs=[hbm] * len(arguments),
+        out_specs=(vmem, vmem, vmem),
         scratch_shapes=scratch,
         compiler_params=pltpu.CompilerParams(
-            collective_id=0, has_side_effects=True, vmem_limit_bytes=40 * 1024 * 1024
+            collective_id=0, has_side_effects=True, vmem_limit_bytes=56 * 1024 * 1024
         ),
         name="density_steps",
-    )(density_map, offsets, velocities, weights, atom_cells, pair_tiles, halo_lists)
+    )(*arguments)
+    speed = speed + push
+    return moved + TIME_STEP * speed, speed
 
 
 def solution(mesh):

time: 90.4 us -> 65.3 us (0.72)
  Pallas kernels: 82.7 us -> 63.2 us
  local copies, waits for them, and re-layouts: 6.25 us -> 0 us
  other arithmetic: 0 us -> 1.33 us
    pallas_call x1, Pallas kernels: 82.7 us -> 63.2 us  [per_device(): pl.pallas_call(kernel, out_shape=(out, out, out), in_specs=[hbm] * len(ar...]
    unnamed x16 -> x0, local copies, waits for them, and re-layouts: 6.25 us -> none
    add x0 -> x1, other arithmetic: none -> 1.33 us  [per_device(): return (moved + TIME_STEP * speed, speed)]
where the time goes in v2:
time: 65.3 us; the launch traced here: 65.1 us
  Pallas kernels  63.2 us (97%)
  other arithmetic  1.33 us (2%)
    pallas_call x1, Pallas kernels, per_device(): pl.pallas_call(kernel, out_shape=(out, out, out), in_specs=[hbm] * len(ar...  63.2 us
    add x1, other arithmetic, per_device(): return (moved + TIME_STEP * speed, speed)  1.33 us

profile of v2, /device:TPU:1, one launch (start us, length us, event | category | flops | bytes accessed | tf_op | source)
XLA Modules:
  0.0 65.1 jit_solution(18385546246287276716)
XLA Ops:
  0.6 63.2 %density_steps.1 = (f32[3,1,1,512]{3,2,1,0:T(1,128)}, f32[3,1,1,512]{3,2,1,0:T(1,128)}, f32[3,1,1,512]{3,2,1,0:T(1,128)}) custom-call(f32[1,512,128]{2,1,0:T(8,128)} %map_hbm.1, f32[3,1,1,512]{3,2,1,0:T(1,128)} %offsets_hbm.1, f32[3,1,1,512]{3,2,1,0:T(1,128)} %velocities_hbm.1, f32[1,1,512]{2,1,0:T(1,128)} %weights_hbm.1, s32[3,1,1,512]{3,2,1,0:T(1,128)} %cells_hbm.1, ...), custom_call_target="tpu_custom_call" | custom-call | tf_op jit(solution)/shard_map/density_steps/pallas_call | solution.py:484
  63.8 1.3 %multiply_add_fusion = (f32[3,1,1,512]{3,2,1,0:T(1,128)}, f32[3,1,1,512]{3,2,1,0:T(1,128)}) fusion(f32[3,1,1,512]{3,2,1,0:T(1,128)} %get-tuple-element.5, f32[3,1,1,512]{3,2,1,0:T(1,128)} %get-tuple-element.6, f32[3,1,1,512]{3,2,1,0:T(1,128)} %get-tuple-element.7), kind=kLoop, calls=%fused_computation | loop fusion | flops 4608 | bytes 30720 | tf_op jit(solution)/shard_map/add | solution.py:496

commit v3 on v2

--- a/solution.py
+++ b/solution.py
@@ -104,11 +104,10 @@
 
     barrier = pltpu.get_barrier_semaphore()
 
-    def greet(k, carry):
-        pl.semaphore_signal(barrier, inc=1, device_id=((dom + k) % DOMAINS, slab), device_id_type=MESH)
-        return carry
-
-    lax.fori_loop(1, DOMAINS, greet, 0)
+    def greet(slot, peer):
+        pl.semaphore_signal(barrier, inc=1, device_id=(peer, slab), device_id_type=MESH)
+
+    for_dom_peers(dom, greet)
     for k in range(1, SLABS):
         pl.semaphore_signal(barrier, inc=1, device_id=(dom, (slab + k) % SLABS), device_id_type=MESH)
 
@@ -226,65 +225,6 @@
             if kind == 0:
                 own_moved = moved
 
-        def spread_half(half, carry):
-            def spread_row(i, carry):
-                r = 1 + half * 7 + i
-                cross = jnp.concatenate(
-                    [
-                        (y_own[pl.ds(r, 1)] * z_near[0]).astype(BF16),
-                        (y_near[half, pl.ds(r, 1)] * z_near[half + 1]).astype(BF16),
-                    ],
-                    axis=1,
-                )
-                out = lax.dot_general(cross, xf_pair[half], (((1,), (1,)), ((), ())), preferred_element_type=F32)
-                place = pl.ds(pl.multiple_of(r * Z_CELLS, Z_CELLS), Z_CELLS)
-                rho[place] = out
-                windows[1, place] = out.astype(BF16)
-                return carry
-
-            return lax.fori_loop(0, 7, spread_row, carry, unroll=7)
-
-        lax.fori_loop(0, 2, spread_half, 0)
-
-        @pl.when(step == 0)
-        def _():
-            everything = map_recv.at[pl.ds(0, DOMAINS - 1)]
-            pltpu.make_async_copy(everything, everything, map_rsem).wait()
-            map_rows[...] = map_recv[...].astype(F32).reshape(X_CELLS * ROWS, Z_CELLS)
-
-            for r in range(ROWS):
-                plane = map_rows[pl.ds(r, X_CELLS, stride=ROWS)]
-                windows[0, r * Z_CELLS : (r + 1) * Z_CELLS] = plane.T.astype(BF16)
-
-        def sum_row(r, carry):
-            rr, rm = carry
-            place = pl.ds(pl.multiple_of(r * Z_CELLS, Z_CELLS), Z_CELLS)
-            here = rho[place].reshape(16, 8, X_CELLS)
-            there = windows[0, place].astype(F32).reshape(16, 8, X_CELLS)
-            return rr + jnp.sum(here * here, axis=0), rm + jnp.sum(here * there, axis=0)
-
-        nothing = jnp.zeros((8, X_CELLS), F32)
-        rr, rm = lax.fori_loop(BELOW, BELOW + Y_CELLS, sum_row, (nothing, nothing))
-        both = jnp.concatenate(
-            [jnp.sum(rr, axis=0, keepdims=True), jnp.sum(rm, axis=0, keepdims=True)], axis=1
-        )
-        both = both + pltpu.roll(both, 96, 1)
-        lane = lax.broadcasted_iota(jnp.int32, (1, 128), 1)
-        sums = jnp.where(lane < 64, both, map_square[...])
-        sums_send[step] = jnp.where((lane >= 32) & (lane < 64), pltpu.roll(both, 96, 1), sums)
-
-        def dom_copy(slot, peer):
-            pltpu.make_async_remote_copy(
-                src_ref=sums_send.at[step],
-                dst_ref=dom_recv.at[step, slot],
-                send_sem=dom_ssem.at[step],
-                recv_sem=dom_rsem.at[step],
-                device_id=(peer, slab),
-                device_id_type=MESH,
-            ).start()
-
-        for_dom_peers(dom, dom_copy)
-
         positions = jnp.concatenate([cell_rows[i] + own_moved[i] for i in range(3)] + [weights] + [zero_row] * 4, axis=0)
         high = positions.astype(BF16).astype(F32)
         middle = (positions - high).astype(BF16).astype(F32)
@@ -309,6 +249,69 @@
         for entry in range(4):
             rim_send[step, entry] = listed[:, entry * HALO : (entry + 1) * HALO]
             rim_copy(entry).start()
+
+        def spread(first, rows, apart):
+            def spread_half(half, carry):
+                def spread_row(i, carry):
+                    r = first + half * apart + i
+                    cross = jnp.concatenate(
+                        [
+                            (y_own[pl.ds(r, 1)] * z_near[0]).astype(BF16),
+                            (y_near[half, pl.ds(r, 1)] * z_near[half + 1]).astype(BF16),
+                        ],
+                        axis=1,
+                    )
+                    out = lax.dot_general(cross, xf_pair[half], (((1,), (1,)), ((), ())), preferred_element_type=F32)
+                    place = pl.ds(pl.multiple_of(r * Z_CELLS, Z_CELLS), Z_CELLS)
+                    rho[place] = out
+                    windows[1, place] = out.astype(BF16)
+                    return carry
+
+                return lax.fori_loop(0, rows, spread_row, carry, unroll=rows)
+
+            lax.fori_loop(0, 2, spread_half, 0)
+
+        spread(BELOW, Y_CELLS // 2, Y_CELLS // 2)
+
+        @pl.when(step == 0)
+        def _():
+            everything = map_recv.at[pl.ds(0, DOMAINS - 1)]
+            pltpu.make_async_copy(everything, everything, map_rsem).wait()
+            map_rows[...] = map_recv[...].astype(F32).reshape(X_CELLS * ROWS, Z_CELLS)
+
+            for r in range(ROWS):
+                plane = map_rows[pl.ds(r, X_CELLS, stride=ROWS)]
+                windows[0, r * Z_CELLS : (r + 1) * Z_CELLS] = plane.T.astype(BF16)
+
+        def sum_row(r, carry):
+            rr, rm = carry
+            place = pl.ds(pl.multiple_of(r * Z_CELLS, Z_CELLS), Z_CELLS)
+            here = rho[place].reshape(16, 8, X_CELLS)
+            there = windows[0, place].astype(F32).reshape(16, 8, X_CELLS)
+            return rr + jnp.sum(here * here, axis=0), rm + jnp.sum(here * there, axis=0)
+
+        nothing = jnp.zeros((8, X_CELLS), F32)
+        rr, rm = lax.fori_loop(BELOW, BELOW + Y_CELLS, sum_row, (nothing, nothing))
+        both = jnp.concatenate(
+            [jnp.sum(rr, axis=0, keepdims=True), jnp.sum(rm, axis=0, keepdims=True)], axis=1
+        )
+        both = both + pltpu.roll(both, 96, 1)
+        lane = lax.broadcasted_iota(jnp.int32, (1, 128), 1)
+        sums = jnp.where(lane < 64, both, map_square[...])
+        sums_send[step] = jnp.where((lane >= 32) & (lane < 64), pltpu.roll(both, 96, 1), sums)
+
+        def dom_copy(slot, peer):
+            pltpu.make_async_remote_copy(
+                src_ref=sums_send.at[step],
+                dst_ref=dom_recv.at[step, slot],
+                send_sem=dom_ssem.at[step],
+                recv_sem=dom_rsem.at[step],
+                device_id=(peer, slab),
+                device_id_type=MESH,
+            ).start()
+
+        for_dom_peers(dom, dom_copy)
+        spread(1, REACH, BELOW + Y_CELLS - 1)
 
         def pull(which, carry):
             def pull_row(r, sums):

time: 65.3 us -> 64.6 us (0.989)
  Pallas kernels: 63.2 us -> 62.4 us
    pallas_call x1, Pallas kernels: 63.2 us -> 62.4 us  [per_device(): pl.pallas_call(kernel, out_shape=(out, out, out), in_specs=[hbm] * len(ar...]
where the time goes in v3:
time: 64.6 us; the launch traced here: 64.4 us
  Pallas kernels  62.4 us (97%)
  other arithmetic  1.33 us (2%)
    pallas_call x1, Pallas kernels, per_device(): pl.pallas_call(kernel, out_shape=(out, out, out), in_specs=[hbm] * len(ar...  62.4 us
    add x1, other arithmetic, per_device(): return (moved + TIME_STEP * speed, speed)  1.33 us

profile of v3, /device:TPU:1, one launch (start us, length us, event | category | flops | bytes accessed | tf_op | source)
XLA Modules:
  0.0 64.4 jit_solution(12685900436090987999)
XLA Ops:
  0.6 62.4 %density_steps.1 = (f32[3,1,1,512]{3,2,1,0:T(1,128)}, f32[3,1,1,512]{3,2,1,0:T(1,128)}, f32[3,1,1,512]{3,2,1,0:T(1,128)}) custom-call(f32[1,512,128]{2,1,0:T(8,128)} %map_hbm.1, f32[3,1,1,512]{3,2,1,0:T(1,128)} %offsets_hbm.1, f32[3,1,1,512]{3,2,1,0:T(1,128)} %velocities_hbm.1, f32[1,1,512]{2,1,0:T(1,128)} %weights_hbm.1, s32[3,1,1,512]{3,2,1,0:T(1,128)} %cells_hbm.1, ...), custom_call_target="tpu_custom_call" | custom-call | tf_op jit(solution)/shard_map/density_steps/pallas_call | solution.py:487
  63.0 1.3 %multiply_add_fusion = (f32[3,1,1,512]{3,2,1,0:T(1,128)}, f32[3,1,1,512]{3,2,1,0:T(1,128)}) fusion(f32[3,1,1,512]{3,2,1,0:T(1,128)} %get-tuple-element.5, f32[3,1,1,512]{3,2,1,0:T(1,128)} %get-tuple-element.6, f32[3,1,1,512]{3,2,1,0:T(1,128)} %get-tuple-element.7), kind=kLoop, calls=%fused_computation | loop fusion | flops 4608 | bytes 30720 | tf_op jit(solution)/shard_map/add | solution.py:499
